TPU v7x, 512 devices: a whole 4x8x8 slice. The times are simulated.
512 devices in a mesh: seq: 64 (over z, y), heads: 8 (over x, core).
Axes of the slice: x: 4, y: 8, z: 8, core: 2. Of those that a mesh axis runs over, the one named last changes fastest.
Arguments:
- self_queries: bfloat16 [8192, 2048], P('seq', 'heads'), may hold values from -200 to 200
- self_keys: bfloat16 [8192, 2048], P('seq', 'heads'), may hold values from -8 to 8
- self_values: bfloat16 [8192, 2048], P('seq', 'heads'), may hold values from -6 to 6
- cross_queries: bfloat16 [8192, 2048], P('seq', 'heads'), may hold values from -200 to 200
- store_keys: bfloat16 [256, 128, 2048], P(None, 'seq', 'heads'), may hold values from -8 to 8
- store_values: bfloat16 [256, 128, 2048], P(None, 'seq', 'heads'), may hold values from -6 to 6
- neighbour_ids: int32 [128, 2], replicated, may hold values from 0 to 255
- out_weight: bfloat16 [2048, 4096], P('heads'), may hold values from -0.125 to 0.125
- grad_out: bfloat16 [8192, 4096], P('seq'), may hold values from -6 to 6
Outputs:
- self_out: bfloat16 [8192, 2048], P('seq', 'heads')
- projected: bfloat16 [8192, 4096], P('seq', 'heads')
- grad_cross_queries: float32 [8192, 2048], P('seq', 'heads')
- grad_store_keys: bfloat16 [256, 128, 2048], P(None, 'seq', 'heads')
- grad_store_values: bfloat16 [256, 128, 2048], P(None, 'seq', 'heads')
All inputs are finite; a program needn't handle non-finite values.
Results may differ from a plain program's by a relative error of at most 0.019.
Values may be sent and summed in bfloat16 or wider, within the bound.
A program may use at most 64 MiB of HBM per device.

v0:
```python
import math

import jax
import jax.numpy as jnp
from jax import lax
from jax.sharding import PartitionSpec as P

HEAD_DIM = 128
SPAN = 64
NEIGH = 2


masked_score = -1e30


def attend_half(
    running, queries, query_position, key_heads, value_heads, key_position, first_row, score_scale
):

    def compute(current):
        top_old, total_old, summed_old = current
        scores = (
            jnp.einsum("qhd,khd->hqk", queries, key_heads, preferred_element_type=jnp.float32)
            * score_scale
        )
        allowed = key_position[None, None, :] <= query_position[None, :, None]
        scores = jnp.where(allowed, scores, masked_score)
        top_new = jnp.maximum(top_old, jnp.max(scores, axis=2))
        numerators = jnp.where(allowed, jnp.exp(scores - top_new[:, :, None]), 0.0)
        total_new = jnp.sum(numerators, axis=2)
        blended = jnp.einsum(
            "hqk,khd->qhd",
            numerators.astype(jnp.bfloat16),
            value_heads,
            preferred_element_type=jnp.float32,
        )
        return (top_new, total_new, blended)

    return lax.cond(first_row <= jnp.max(query_position), compute, lambda current: current, running)


def shards(
    self_queries,
    self_keys,
    self_values,
    cross_queries,
    store_keys,
    store_values,
    neighbour_ids,
    out_weight,
    grad_out,
):
    seq_count = lax.axis_size("seq")
    seq_index = lax.axis_index("seq")
    local_tokens = self_queries.shape[0]
    full_width = self_queries.shape[1]
    head_count = full_width // HEAD_DIM
    half_tokens = local_tokens // 2
    score_scale = 1.0 / math.sqrt(HEAD_DIM)
    offsets = jnp.arange(half_tokens, dtype=jnp.int32)
    lower_rows = self_queries[:half_tokens]
    upper_rows = self_queries[half_tokens:]
    lower_position = seq_index * local_tokens + offsets
    upper_position = seq_index * local_tokens + half_tokens + offsets
    lower_heads = lower_rows.reshape(half_tokens, head_count, HEAD_DIM)
    upper_heads = upper_rows.reshape(half_tokens, head_count, HEAD_DIM)

    def empty_state():
        return (
            jnp.full((head_count, half_tokens), masked_score, jnp.float32),
            jnp.zeros((head_count, half_tokens), jnp.float32),
            jnp.zeros((half_tokens, head_count, HEAD_DIM), jnp.float32),
        )

    first_row = jnp.int32(0)
    key_rows = lax.all_gather(self_keys, "seq", axis=0, tiled=True)
    value_rows = lax.all_gather(self_values, "seq", axis=0, tiled=True)
    row_count = key_rows.shape[0]
    key_position = jnp.arange(row_count, dtype=jnp.int32)
    key_heads = key_rows.reshape(row_count, head_count, HEAD_DIM)
    value_heads = value_rows.reshape(row_count, head_count, HEAD_DIM)
    lower_state = attend_half(
        empty_state(),
        lower_heads,
        lower_position,
        key_heads,
        value_heads,
        key_position,
        first_row,
        score_scale,
    )
    upper_state = attend_half(
        empty_state(),
        upper_heads,
        upper_position,
        key_heads,
        value_heads,
        key_position,
        first_row,
        score_scale,
    )
    lower_state, upper_state = (lower_state, upper_state)

    def finish(state):
        normed = state[2] / jnp.transpose(state[1])[:, :, None]
        return normed.reshape(half_tokens, full_width).astype(jnp.bfloat16)

    lower_out = finish(lower_state)
    upper_out = finish(upper_state)
    self_out = jnp.concatenate([lower_out, upper_out], axis=0)
    spans_here = local_tokens // SPAN
    grad_cross = lax.dot_general(
        grad_out, out_weight, (((1,), (1,)), ((), ())), preferred_element_type=jnp.float32
    )
    grad_rounded = grad_cross.astype(jnp.bfloat16)
    group_count = spans_here + 1
    padded_ids = jnp.concatenate([jnp.zeros((1, NEIGH), jnp.int32), neighbour_ids], axis=0)
    requester = (
        jnp.arange(seq_count, dtype=jnp.int32)[:, None] * spans_here
        + jnp.arange(group_count, dtype=jnp.int32)[None, :]
    )
    wanted = padded_ids[requester]

    def grouped(rows, front):
        pad_back = jnp.zeros((SPAN - 1, full_width), rows.dtype)
        joined = jnp.concatenate([front, rows, pad_back], axis=0)
        return joined.reshape(group_count, SPAN, head_count, HEAD_DIM)

    zero_row = jnp.zeros((1, full_width), jnp.bfloat16)
    query_groups = grouped(cross_queries, zero_row)
    grad_groups = grouped(grad_rounded, zero_row)
    global_place = seq_index * local_tokens + jnp.arange(group_count * SPAN, dtype=jnp.int32)
    row_live = global_place >= SPAN
    matched = row_live.astype(jnp.float32).reshape(group_count, SPAN, 1, 1)
    grad_groups = (grad_groups * matched).astype(jnp.bfloat16)
    send_keys = store_keys[wanted]
    send_values = store_values[wanted]
    got_keys, got_values = (
        lax.all_to_all(send_keys, "seq", split_axis=0, concat_axis=3, tiled=True),
        lax.all_to_all(send_values, "seq", split_axis=0, concat_axis=3, tiled=True),
    )
    near_rows = NEIGH * got_keys.shape[3]
    fetched_keys = got_keys.reshape(group_count, near_rows, head_count, HEAD_DIM)
    fetched_values = got_values.reshape(group_count, near_rows, head_count, HEAD_DIM)
    scores = (
        jnp.einsum(
            "gqhd,gkhd->ghqk", query_groups, fetched_keys, preferred_element_type=jnp.float32
        )
        * score_scale
    )
    row_max = jnp.max(scores, axis=3, keepdims=True)
    numerators = jnp.exp(scores - row_max)
    cross_share = numerators / jnp.sum(numerators, axis=3, keepdims=True)
    rounded_share = cross_share.astype(jnp.bfloat16)
    cross_out = jnp.einsum(
        "ghqk,gkhd->gqhd", rounded_share, fetched_values, preferred_element_type=jnp.float32
    )
    cross_out = (cross_out * matched).astype(jnp.bfloat16)
    grad_share = jnp.einsum(
        "gqhd,gkhd->ghqk", grad_groups, fetched_values, preferred_element_type=jnp.float32
    )
    grad_scores = cross_share * (
        grad_share - jnp.sum(cross_share * grad_share, axis=3, keepdims=True)
    )
    rounded_grads = grad_scores.astype(jnp.bfloat16)
    query_grads = (
        jnp.einsum(
            "ghqk,gkhd->gqhd", rounded_grads, fetched_keys, preferred_element_type=jnp.float32
        )
        * score_scale
    )
    key_grads = (
        jnp.einsum(
            "ghqk,gqhd->gkhd", rounded_grads, query_groups, preferred_element_type=jnp.float32
        )
        * score_scale
    )
    value_grads = jnp.einsum(
        "ghqk,gqhd->gkhd", rounded_share, grad_groups, preferred_element_type=jnp.float32
    )
    owner_rows = store_keys.shape[1]
    key_back = key_grads.reshape(group_count, NEIGH, seq_count, owner_rows, full_width)
    value_back = value_grads.reshape(group_count, NEIGH, seq_count, owner_rows, full_width)
    back_keys, back_values = (
        lax.all_to_all(
            key_back.astype(jnp.bfloat16), "seq", split_axis=2, concat_axis=0, tiled=True
        ).astype(key_back.dtype),
        lax.all_to_all(
            value_back.astype(jnp.bfloat16), "seq", split_axis=2, concat_axis=0, tiled=True
        ).astype(value_back.dtype),
    )
    flat_wanted = wanted.reshape(seq_count * group_count * NEIGH)
    selector = (
        jnp.arange(store_keys.shape[0], dtype=jnp.int32)[:, None] == flat_wanted[None, :]
    ).astype(jnp.float32)
    grad_store_keys = jnp.dot(
        selector,
        back_keys.reshape(flat_wanted.shape[0], owner_rows * full_width),
        precision=lax.Precision.HIGHEST,
        preferred_element_type=jnp.float32,
    )
    grad_store_values = jnp.dot(
        selector,
        back_values.reshape(flat_wanted.shape[0], owner_rows * full_width),
        precision=lax.Precision.HIGHEST,
        preferred_element_type=jnp.float32,
    )
    grad_store_keys = grad_store_keys.reshape(store_keys.shape).astype(jnp.bfloat16)
    grad_store_values = grad_store_values.reshape(store_values.shape).astype(jnp.bfloat16)
    cross_flat = cross_out.reshape(group_count * SPAN, full_width)
    query_flat = query_grads.reshape(group_count * SPAN, full_width)
    cross_rows = cross_flat[1 : local_tokens + 1]
    grad_cross_queries = query_flat[1 : local_tokens + 1]
    projected_part = lax.psum_scatter(
        lax.dot_general(
            out_weight, cross_rows, (((0,), (1,)), ((), ())), preferred_element_type=jnp.float32
        ).astype(jnp.bfloat16),
        "heads",
        scatter_dimension=0,
        tiled=True,
    ).astype(jnp.float32)
    projected = jnp.transpose(projected_part).astype(jnp.bfloat16)
    return (self_out, projected, grad_cross_queries, grad_store_keys, grad_store_values)


def solution(mesh):
    in_specs = (
        P("seq", "heads"),
        P("seq", "heads"),
        P("seq", "heads"),
        P("seq", "heads"),
        P(None, "seq", "heads"),
        P(None, "seq", "heads"),
        P(),
        P("heads", None),
        P("seq", None),
    )
    out_specs = (
        P("seq", "heads"),
        P("seq", "heads"),
        P("seq", "heads"),
        P(None, "seq", "heads"),
        P(None, "seq", "heads"),
    )
    return jax.shard_map(shards, mesh=mesh, in_specs=in_specs, out_specs=out_specs, check_vma=False)
```

profile of v0, /device:TPU:14, one launch (start us, length us, event | category | flops | bytes accessed | tf_op | source)
XLA Modules:
  0.0 250.6 jit_solution(909491567552229502)
XLA Ops:
  8.1 1.7 copy.54
  14.2 3.3 %gather_fusion.1 = bf16[384,2,256]{2,1,0:T(2,128)(2,1)} fusion(bf16[256,2,256]{2,1,0:T(2,128)(2,1)} %param.18, s32[1024]{0:T(1024)S(1)} %pad_clamp_fusion), kind=kCustom, calls=%fused_computation.1 | custom fusion | bytes 787968 | tf_op jit(solution)/shard_map/gather | solution.py:137
  17.5 16.6 %all-to-all-start = ((bf16[64,3,2,2,256]{4,3,2,1,0:T(2,128)(2,1)}), bf16[64,3,2,2,256]{4,3,2,1,0:T(2,128)(2,1)S(1)}, u32[]{:S(2)}, u32[]{:S(2)}) async-start(bf16[64,3,2,2,256]{4,3,2,1,0:T(2,128)(2,1)} %bitcast.6), calls=%async_computation | async-start | bytes 786432 | tf_op jit(solution)/shard_map/all_to_all | solution.py:140
  34.1 3.0 %gather_fusion.2 = bf16[384,2,256]{2,1,0:T(2,128)(2,1)} fusion(bf16[256,2,256]{2,1,0:T(2,128)(2,1)S(1)} %copy-done.4, s32[1024]{0:T(1024)S(1)} %pad_clamp_fusion), kind=kCustom, calls=%fused_computation.2 | custom fusion | bytes 787968 | tf_op jit(solution)/shard_map/gather | solution.py:136
  37.0 14.9 %all-to-all-done = bf16[64,3,2,2,256]{4,3,2,1,0:T(2,128)(2,1)S(1)} async-done(((bf16[64,3,2,2,256]{4,3,2,1,0:T(2,128)(2,1)}), bf16[64,3,2,2,256]{4,3,2,1,0:T(2,128)(2,1)S(1)}, u32[]{:S(2)}, u32[]{:S(2)}) %all-to-all-start) | async-done | bytes 393248 | tf_op jit(solution)/shard_map/all_to_all | solution.py:140
  51.9 5.2 %all-to-all-start.1 = ((bf16[64,3,2,2,256]{4,3,2,1,0:T(2,128)(2,1)}), bf16[64,3,2,2,256]{4,3,2,1,0:T(2,128)(2,1)S(1)}, u32[]{:S(2)}, u32[]{:S(2)}) async-start(bf16[64,3,2,2,256]{4,3,2,1,0:T(2,128)(2,1)} %bitcast.9), calls=%async_computation.1 | async-start | bytes 786432 | tf_op jit(solution)/shard_map/all_to_all | solution.py:139
  57.2 2.1 convolution_convert_fusion.4
  62.2 11.0 %all-to-all-done.1 = bf16[64,3,2,2,256]{4,3,2,1,0:T(2,128)(2,1)S(1)} async-done(((bf16[64,3,2,2,256]{4,3,2,1,0:T(2,128)(2,1)}), bf16[64,3,2,2,256]{4,3,2,1,0:T(2,128)(2,1)S(1)}, u32[]{:S(2)}, u32[]{:S(2)}) %all-to-all-start.1) | async-done | bytes 393248 | tf_op jit(solution)/shard_map/all_to_all | solution.py:139
  75.9 1.8 fusion.37
  80.1 2.0 fusion.34
  84.4 2.0 copy.77
  86.4 5.2 %all-to-all-start.2 = ((bf16[3,2,64,2,256]{4,3,1,0,2:T(2,128)(2,1)}), bf16[3,2,64,2,256]{4,3,1,0,2:T(2,128)(2,1)S(1)}, u32[]{:S(2)}, u32[]{:S(2)}) async-start(bf16[3,2,64,2,256]{4,3,1,0,2:T(2,128)(2,1)} %copy.77), calls=%async_computation.3 | async-start | bytes 786432 | tf_op jit(solution)/shard_map/all_to_all | solution.py:185
  91.7 2.4 fusion.29
  94.1 2.8 %fusion.32 = bf16[3,256,2,128]{1,3,2,0:T(8,128)(2,1)} fusion(f32[3,64,2,128]{3,2,1,0:T(2,128)} %reshape.217, f32[3,64]{1,0:T(4,128)S(1)} %fusion.58, f32[3,2,64]{2,1,0:T(2,128)S(1)} %get-tuple-element.88, f32[3,2,64,256]{3,2,1,0:T(8,128)S(1)} %convolution_multiply_fusion.3), kind=kOutput, calls=%fused_computation.42 | convolution fusion | flops 25756288 | bytes 985344 | tf_op jit(solution)/shard_map/ghqk,gqhd->gkhd/dot_general | solution.py:178
  99.1 2.0 copy.80
  101.2 9.3 %all-to-all-done.2 = bf16[3,2,64,2,256]{4,3,1,0,2:T(2,128)(2,1)S(1)} async-done(((bf16[3,2,64,2,256]{4,3,1,0,2:T(2,128)(2,1)}), bf16[3,2,64,2,256]{4,3,1,0,2:T(2,128)(2,1)S(1)}, u32[]{:S(2)}, u32[]{:S(2)}) %all-to-all-start.2) | async-done | bytes 393248 | tf_op jit(solution)/shard_map/all_to_all | solution.py:185
  110.4 6.3 %all-to-all-start.3 = ((bf16[3,2,64,2,256]{4,3,1,0,2:T(2,128)(2,1)}), bf16[3,2,64,2,256]{4,3,1,0,2:T(2,128)(2,1)S(1)}, u32[]{:S(2)}, u32[]{:S(2)}) async-start(bf16[3,2,64,2,256]{4,3,1,0,2:T(2,128)(2,1)} %copy.80), calls=%async_computation.4 | async-start | bytes 786432 | tf_op jit(solution)/shard_map/all_to_all | solution.py:188
  122.4 13.1 %all-to-all-done.3 = bf16[3,2,64,2,256]{4,3,1,0,2:T(2,128)(2,1)S(1)} async-done(((bf16[3,2,64,2,256]{4,3,1,0,2:T(2,128)(2,1)}), bf16[3,2,64,2,256]{4,3,1,0,2:T(2,128)(2,1)S(1)}, u32[]{:S(2)}, u32[]{:S(2)}) %all-to-all-start.3) | async-done | bytes 393248 | tf_op jit(solution)/shard_map/all_to_all | solution.py:188
  137.0 89.5 %all-gather.5.cloned.1.call-done = bf16[8192,256]{0,1:T(8,128)(2,1)} async-done(((bf16[128,256]{0,1:T(8,128)(2,1)}), bf16[8192,256]{0,1:T(8,128)(2,1)}) %all-gather.5.cloned.1.call-update) | async-done | bytes 4194320 | tf_op jit(solution)/shard_map/all_gather | solution.py:77
  226.6 7.9 %conditional.3 = (f32[2,64]{1,0:T(2,128)S(1)}, f32[64,2,128]{2,0,1:T(8,128)S(1)}) conditional(s32[]{:T(128)} %convert_element_type.96, () %tuple.26, (s32[8192]{0:T(1024)S(1)}, s32[64]{0:T(128)S(1)}, bf16[128,256]{1,0:T(8,128)(2,1)S(1)}, bf16[8192,2,128]{0,2,1:T(8,128)(2,1)}, bf16[8192,2,128]{0,2,1:T(8,128)(2,1)}) %tuple.56), branch_computations={%region_6.7_spmd, %region_7.10_spmd} | conditional | flops 546832256 | bytes 39980332 | solution.py:39
  227.0 3.7 %fusion.62 = (f32[2,64]{1,0:T(2,128)S(1)}, f32[2,64,8192]{2,1,0:T(8,128)S(1)}) fusion(bf16[8192,2,128]{0,2,1:T(8,128)(2,1)} %get-tuple-element.75, pred[64,8192]{1,0:T(8,128)(4,1)S(1)} %broadcast_compare_fusion.1, bf16[128,256]{1,0:T(8,128)(2,1)S(1)} %get-tuple-element.31), kind=kOutput, calls=%fused_computation.96 | convolution fusion | flops 271581056 | bytes 8946176 | tf_op jit(solution)/shard_map/cond/branch_1_fun/qhd,khd->hqk/dot_general | solution.py:23
  234.5 7.8 %conditional.2 = (f32[2,64]{1,0:T(2,128)S(1)}, f32[64,2,128]{2,0,1:T(8,128)S(1)}) conditional(s32[]{:T(128)} %convert_element_type.93, () %tuple.24, (s32[8192]{0:T(1024)S(1)}, s32[64]{0:T(128)S(1)}, bf16[128,256]{1,0:T(8,128)(2,1)S(1)}, bf16[8192,2,128]{0,2,1:T(8,128)(2,1)}, bf16[8192,2,128]{0,2,1:T(8,128)(2,1)}) %tuple.57), branch_computations={%region_1.0_spmd, %region_2.5_spmd} | conditional | flops 546832256 | bytes 39980332 | solution.py:39
  234.8 3.7 %fusion.61 = (f32[2,64]{1,0:T(2,128)S(1)}, f32[2,64,8192]{2,1,0:T(8,128)S(1)}) fusion(bf16[8192,2,128]{0,2,1:T(8,128)(2,1)} %get-tuple-element.70, pred[64,8192]{1,0:T(8,128)(4,1)S(1)} %broadcast_compare_fusion, bf16[128,256]{1,0:T(8,128)(2,1)S(1)} %get-tuple-element.26), kind=kOutput, calls=%fused_computation.95 | convolution fusion | flops 271581056 | bytes 8946176 | tf_op jit(solution)/shard_map/cond/branch_1_fun/qhd,khd->hqk/dot_general | solution.py:23
  240.7 1.6 fusion.8
  (85 shorter events, 30.4 us)
Async XLA Ops:
  8.0 49.2 %copy-start = (bf16[256,4096]{1,0:T(8,128)(2,1)S(1)}, bf16[256,4096]{1,0:T(8,128)(2,1)}, u32[]{:S(2)}) copy-start(bf16[256,4096]{1,0:T(8,128)(2,1)} %param.20) | copy-start | bytes 6291460
  8.0 26.0 %copy-start.4 = (bf16[256,2,256]{2,1,0:T(2,128)(2,1)S(1)}, bf16[256,2,256]{2,1,0:T(2,128)(2,1)}, u32[]{:S(2)}) copy-start(bf16[256,2,256]{2,1,0:T(2,128)(2,1)} %param.17) | copy-start | bytes 786436
  8.0 129.0 %all-gather.3.cloned.1.call-start = ((), (), s32[]{:S(2)}) async-start(), calls=%async_computation.5 | async-start | bytes 4259840 | tf_op jit(solution)/shard_map/all_gather | solution.py:76
  9.8 216.7 %all-gather.5.cloned.1.call-start = ((), (), s32[]{:S(2)}) async-start(), calls=%async_computation.6 | async-start | bytes 4259840 | tf_op jit(solution)/shard_map/all_gather | solution.py:77
  12.5 46.8 %copy-start.6 = (bf16[128,256]{1,0:T(8,128)(2,1)S(1)}, bf16[128,256]{1,0:T(8,128)(2,1)}, u32[]{:S(2)}) copy-start(bf16[128,256]{1,0:T(8,128)(2,1)} %param.16) | copy-start | bytes 196612
  13.2 4.2 %copy-start.3 = (s32[192,2]{1,0:T(8,128)}, s32[192,2]{1,0:T(8,128)S(1)}, u32[]{:S(2)}) copy-start(s32[192,2]{1,0:T(8,128)S(1)} %gather_fusion) | copy-start | bytes 4612
  17.5 34.5 %all-to-all-start = ((bf16[64,3,2,2,256]{4,3,2,1,0:T(2,128)(2,1)}), bf16[64,3,2,2,256]{4,3,2,1,0:T(2,128)(2,1)S(1)}, u32[]{:S(2)}, u32[]{:S(2)}) async-start(bf16[64,3,2,2,256]{4,3,2,1,0:T(2,128)(2,1)} %bitcast.6), calls=%async_computation | async-start | bytes 786432 | tf_op jit(solution)/shard_map/all_to_all | solution.py:140
  51.9 21.2 %all-to-all-start.1 = ((bf16[64,3,2,2,256]{4,3,2,1,0:T(2,128)(2,1)}), bf16[64,3,2,2,256]{4,3,2,1,0:T(2,128)(2,1)S(1)}, u32[]{:S(2)}, u32[]{:S(2)}) async-start(bf16[64,3,2,2,256]{4,3,2,1,0:T(2,128)(2,1)} %bitcast.9), calls=%async_computation.1 | async-start | bytes 786432 | tf_op jit(solution)/shard_map/all_to_all | solution.py:139
  86.4 24.0 %all-to-all-start.2 = ((bf16[3,2,64,2,256]{4,3,1,0,2:T(2,128)(2,1)}), bf16[3,2,64,2,256]{4,3,1,0,2:T(2,128)(2,1)S(1)}, u32[]{:S(2)}, u32[]{:S(2)}) async-start(bf16[3,2,64,2,256]{4,3,1,0,2:T(2,128)(2,1)} %copy.77), calls=%async_computation.3 | async-start | bytes 786432 | tf_op jit(solution)/shard_map/all_to_all | solution.py:185
  91.6 151.5 %reduce-scatter.2.cloned.1.call-start = ((), (), s32[]{:S(2)}) async-start(), calls=%async_computation.7 | async-start | bytes 1179648 | tf_op jit(solution)/shard_map/reduce_scatter | solution.py:214
  101.2 125.4 %copy-start.5 = (bf16[128,256]{1,0:T(8,128)(2,1)S(1)}, bf16[128,256]{1,0:T(8,128)(2,1)}, u32[]{:S(2)}) copy-start(bf16[128,256]{1,0:T(8,128)(2,1)} %param.13) | copy-start | bytes 196612
  110.4 25.0 %all-to-all-start.3 = ((bf16[3,2,64,2,256]{4,3,1,0,2:T(2,128)(2,1)}), bf16[3,2,64,2,256]{4,3,1,0,2:T(2,128)(2,1)S(1)}, u32[]{:S(2)}, u32[]{:S(2)}) async-start(bf16[3,2,64,2,256]{4,3,1,0,2:T(2,128)(2,1)} %copy.80), calls=%async_computation.4 | async-start | bytes 786432 | tf_op jit(solution)/shard_map/all_to_all | solution.py:188
  230.7 2.2 copy-start.1
  238.5 2.2 copy-start.2
Sparse Core Ops, SparseCore 0:
  12.4 120.3 all-gather.2
  135.8 90.7 all-gather.4
Sparse Core Ops, SparseCore 1:
  95.5 35.4 reduce-scatter.1
where the time goes:
time: 252 us; the launch traced here: 251 us
  waiting for transfers between devices  138 us (55%)
  starting transfers between devices  33.3 us (13%)
  local copies, waits for them, and re-layouts  31.2 us (12%)
  matrix products  25.1 us (10%)
  between operations  17.1 us (7%)
  other arithmetic  6.02 us (2%)
    all_gather x1, waiting for transfers between devices, shards(): value_rows = lax.all_gather(self_values, 'seq', axis=0, tiled=True)  89.5 us
    all_to_all x1, starting transfers between devices, shards(): lax.all_to_all(send_values, 'seq', split_axis=0, concat_axis=3, tiled=True)  16.6 us
    all_to_all x1, waiting for transfers between devices, shards(): lax.all_to_all(send_values, 'seq', split_axis=0, concat_axis=3, tiled=True)  14.9 us
    all_to_all x1, waiting for transfers between devices, shards(): lax.all_to_all(value_back.astype(jnp.bfloat16), 'seq', split_axis=2, conc...  13.1 us
    all_to_all x1, waiting for transfers between devices, shards(): lax.all_to_all(send_keys, 'seq', split_axis=0, concat_axis=3, tiled=True)  11 us
    all_to_all x1, waiting for transfers between devices, shards(): lax.all_to_all(key_back.astype(jnp.bfloat16), 'seq', split_axis=2, concat...  9.27 us
    dot_general x2, matrix products, compute(): jnp.einsum('qhd,khd->hqk', queries, key_heads, preferred_element_type=jnp...  7.37 us
    unnamed x19, local copies, waits for them, and re-layouts  6.85 us
  transfers between devices with their start and end apart: 7, of which 5 were waited for; matrix products, arithmetic and copies ran while one was open for 23% of the time, Pallas kernels for 0%

commit v1 on v0

v1 whole, which is shorter than its diff:
```python
import functools
import math

import jax
import jax.numpy as jnp
from jax import lax
from jax.experimental import pallas as pl
from jax.experimental.pallas import tpu as pltpu
from jax.sharding import PartitionSpec as P

MESH = pl.DeviceIdType.MESH
BF16 = jnp.bfloat16
F32 = jnp.float32
HEAD_DIM = 128
SCALE = 1.0 / math.sqrt(HEAD_DIM)
LOW = -1e30
Z_CHUNKS = 4
Y_CHUNKS = 2


def dot(a, b, dims):
    return lax.dot_general(a, b, (dims, ((), ())), preferred_element_type=F32)


def iota(shape, axis):
    return lax.broadcasted_iota(jnp.int32, shape, axis)


def remote(src, dst, send_sem, recv_sem, device):
    return pltpu.make_async_remote_copy(
        src_ref=src,
        dst_ref=dst,
        send_sem=send_sem,
        recv_sem=recv_sem,
        device_id=device,
        device_id_type=MESH,
    )


def shifted_seq(s, dz, dy):
    return lax.rem(s // 8 + dz, 8) * 8 + lax.rem(lax.rem(s, 8) + dy, 8)


class Ring:
    def __init__(self, buf, send_sem, recv_sem, right, left, chunks):
        self.buf, self.send_sem, self.recv_sem = buf, send_sem, recv_sem
        self.right, self.left, self.chunks = right, left, chunks
        self.rows = buf.shape[1] // chunks

    def copy(self, step, rightward, chunk):
        source, target = (step - 1, step) if rightward else ((9 - step) % 8, 8 - step)
        rows = pl.ds(chunk * self.rows, self.rows)
        return remote(
            self.buf.at[source, rows],
            self.buf.at[target, rows],
            self.send_sem.at[int(rightward), step, chunk],
            self.recv_sem.at[int(rightward), step, chunk],
            self.right if rightward else self.left,
        )

    def moves(self, step):
        half = self.chunks // 2
        return [
            (rightward, chunk)
            for chunk in range(self.chunks)
            for rightward in (True, False)
            if step < 4 or (chunk < half) == rightward
        ]

    def run_step(self, step):
        for rightward, chunk in self.moves(step):
            if step > 1:
                self.copy(step - 1, rightward, chunk).wait_recv()
            self.copy(step, rightward, chunk).start()

    def finish(self):
        for rightward, chunk in self.moves(4):
            self.copy(4, rightward, chunk).wait_recv()
        for rightward, chunk in self.moves(3):
            if (rightward, chunk) not in self.moves(4):
                self.copy(3, rightward, chunk).wait_recv()
        for step in range(1, 5):
            for rightward, chunk in self.moves(step):
                self.copy(step, rightward, chunk).wait_send()


def body(
    sq_in, sk_in, sv_in, cq_in, stk_in, stv_in, idt, w_in, go_in,
    self_out, projected, grad_q, grad_k, grad_v,
    kv, qb, cq, stk, stv, w, go,
    sel_t, sb, rb, gs, gr, gc, shift_s, shift_r, back_s, back_r,
    acc, top, total, o_s, o_r, stat_s, stat_r, part_s, part_r,
    load_sem, z_ss, z_rs, y_ss, y_rs, sems,
):
    s, h = lax.axis_index("seq"), lax.axis_index("heads")
    z, y = s // 8, lax.rem(s, 8)

    def load(i, src, dst):
        return pltpu.make_async_copy(src, dst, load_sem.at[i])

    loads = [
        load(0, stk_in, stk),
        load(1, stv_in, stv),
        load(2, go_in, go),
        load(3, w_in, w),
        load(4, sk_in, kv.at[0, pl.ds(0, 128)]),
        load(5, sv_in, kv.at[0, pl.ds(128, 128)]),
        load(6, sq_in, qb.at[0]),
        load(7, cq_in, cq),
    ]
    for copy in loads:
        copy.start()

    barrier = pltpu.get_barrier_semaphore()

    def greet_seq(k, _):
        device = (shifted_seq(s, k // 8, lax.rem(k, 8)), h)
        pl.semaphore_signal(barrier, inc=1, device_id=device, device_id_type=MESH)
        return 0

    def greet_heads(k, _):
        device = (s, lax.rem(h + k, 8))
        pl.semaphore_signal(barrier, inc=1, device_id=device, device_id_type=MESH)
        return 0

    lax.fori_loop(1, 64, greet_seq, 0)
    lax.fori_loop(1, 8, greet_heads, 0)

    ids = idt[...].astype(F32)
    first_id = jnp.broadcast_to(ids[0:1], (128, 128)).astype(BF16)
    second_id = jnp.broadcast_to(ids[1:2], (128, 128)).astype(BF16)
    sub, lane = iota((512, 128), 0), iota((512, 128), 1)
    span_of = (lane == (((sub >> 2) + 127) & 127)).astype(F32).astype(BF16)
    picked = jnp.where(
        (sub & 2) == 0,
        dot(span_of, first_id, ((1,), (1,))),
        dot(span_of, second_id, ((1,), (1,))),
    )
    wanted = picked * 2.0 + (sub & 1).astype(F32)
    lane_f = lane.astype(F32)
    sel = jnp.concatenate(
        [jnp.where(wanted == lane_f + 128.0 * c, 1.0, 0.0).astype(BF16) for c in range(4)], axis=1
    )
    loads[0].wait()
    keys_out = dot(sel, stk[...].reshape(512, 256), ((1,), (0,)))
    loads[1].wait()
    values_out = dot(sel, stv[...].reshape(512, 256), ((1,), (0,)))
    sb[...] = jnp.concatenate(
        [keys_out.reshape(64, 8, 256), values_out.reshape(64, 8, 256)], axis=1
    ).astype(BF16)
    rb[pl.ds(s, 1)] = sb[pl.ds(s, 1)]

    loads[2].wait()
    loads[3].wait()
    gc[...] = dot(go[...], w[...], ((1,), (1,))).astype(BF16)
    loads[7].wait()
    shift_s[pl.ds(0, 16)] = cq[pl.ds(112, 16)]
    shift_s[pl.ds(16, 16)] = gc[pl.ds(112, 16)]
    loads[4].wait()
    loads[5].wait()
    loads[6].wait()

    pl.semaphore_wait(barrier, 70)

    def start_all(source, target, which):
        def one(k, _):
            to = shifted_seq(s, k // 8, lax.rem(k, 8))
            remote(source.at[to], target.at[s], sems.at[which], sems.at[which + 1], (to, h)).start()
            return 0

        lax.fori_loop(1, 64, one, 0)

    def wait_all(source, target, which):
        rows = pl.ds(0, 63)
        remote(
            source.at[rows],
            target.at[rows],
            sems.at[which],
            sems.at[which + 1],
            (shifted_seq(s, 0, 1), h),
        ).wait()

    after = (lax.rem(s + 1, 64), h)
    before = (lax.rem(s + 63, 64), h)
    ahead = remote(shift_s, shift_r, sems.at[0], sems.at[1], after)
    ahead.start()
    start_all(sb, rb, 2)
    z_ring = Ring(
        kv, z_ss, z_rs, (shifted_seq(s, 1, 0), h), (shifted_seq(s, 7, 0), h), Z_CHUNKS
    )
    y_ring = Ring(
        qb, y_ss, y_rs, (shifted_seq(s, 0, 1), h), (shifted_seq(s, 0, 7), h), Y_CHUNKS
    )
    for step in range(1, 5):
        z_ring.run_step(step)
        y_ring.run_step(step)

    sub_w, lane_w = iota((128, 512), 0), iota((128, 512), 1)
    span_row = (sub_w == (((lane_w >> 2) + 127) & 127)).astype(F32).astype(BF16)
    lane_8 = iota((8, 512), 1)
    picked_row = jnp.where(
        (lane_8 & 2) == 0,
        dot(first_id[0:8], span_row, ((1,), (0,))),
        dot(second_id[0:8], span_row, ((1,), (0,))),
    )
    wanted_row = (picked_row * 2.0 + (lane_8 & 1).astype(F32))[0:1]
    sel_t[...] = jnp.where(iota((512, 512), 0).astype(F32) == wanted_row, 1.0, 0.0).astype(BF16)

    ahead.wait()
    row_1 = iota((128, 256), 0)
    shifted_in = shift_r[...].astype(F32)
    queries = jnp.where(
        row_1 == 0, shifted_in[15:16], pltpu.roll(cq[...].astype(F32), 1, 0)
    ).astype(BF16)
    place = row_1 + s * 128
    unmatched = (place >= 1) & (place < 64)
    grads = jnp.where(row_1 == 0, shifted_in[31:32], pltpu.roll(gc[...].astype(F32), 1, 0))
    grads = jnp.where(unmatched, 0.0, grads).astype(BF16)
    wait_all(sb, rb, 2)
    got = rb[...].astype(F32)
    near_keys = got[:, :8].reshape(512, 256).astype(BF16)
    near_values = got[:, 8:].reshape(512, 256).astype(BF16)
    mine = ((iota((512, 128), 0) & 4) != 0) == (iota((512, 128), 1) >= 64)
    outs, query_grads, key_grads, value_grads = [], [], [], []
    for head in range(2):
        cols = slice(head * 128, head * 128 + 128)
        k_h, v_h, q_h, g_h = near_keys[:, cols], near_values[:, cols], queries[:, cols], grads[:, cols]
        scores = jnp.where(mine, dot(k_h, q_h, ((1,), (1,))) * SCALE, LOW)
        numer = jnp.exp(scores - jnp.max(scores, axis=0, keepdims=True))
        probs = numer / jnp.sum(numer, axis=0, keepdims=True)
        weights = probs.astype(BF16)
        outs.append(dot(weights, v_h, ((0,), (0,))))
        grad_probs = dot(v_h, g_h, ((1,), (1,)))
        centre = jnp.sum(probs * grad_probs, axis=0, keepdims=True)
        grad_weights = (probs * (grad_probs - centre)).astype(BF16)
        query_grads.append(dot(grad_weights, k_h, ((0,), (0,))) * SCALE)
        key_grads.append(dot(grad_weights, q_h, ((1,), (0,))) * SCALE)
        value_grads.append(dot(weights, g_h, ((1,), (0,))))
    key_grads = jnp.concatenate(key_grads, axis=1).reshape(64, 8, 256)
    value_grads = jnp.concatenate(value_grads, axis=1).reshape(64, 8, 256)
    gs[...] = jnp.concatenate([key_grads, value_grads], axis=1).astype(BF16)
    gr[pl.ds(s, 1)] = gs[pl.ds(s, 1)]
    start_all(gs, gr, 4)
    cross = jnp.where(unmatched, 0.0, jnp.concatenate(outs, axis=1))
    query_grads = jnp.concatenate(query_grads, axis=1)
    back_s[...] = jnp.concatenate([cross[0:8], query_grads[0:8]], axis=1)
    back = remote(back_s, back_r, sems.at[6], sems.at[7], before)
    back.start()

    z_ring.finish()
    y_ring.finish()

    def attend(d, first):
        for head in range(2):
            cols = pl.ds(head * 128, 128)
            k_h = kv[pl.ds(d, 1), pl.ds(0, 128), cols].reshape(128, 128)
            v_h = kv[pl.ds(d, 1), pl.ds(128, 128), cols].reshape(128, 128)
            q_h = qb[:, :, cols].reshape(1024, 128)
            scores = dot(k_h, q_h, ((1,), (1,))) * SCALE
            if first:
                key, query = iota((128, 1024), 0), iota((128, 1024), 1)
                block = query >> 7
                allowed = ((block == 0) & (key <= query)) | (block > y)
                scores = jnp.where(allowed, scores, LOW)
                top_new = jnp.max(scores, axis=0, keepdims=True)
                numer = jnp.where(allowed, jnp.exp(scores - top_new), 0.0)
                total[head] = jnp.sum(numer, axis=0, keepdims=True)
                acc[head] = dot(v_h, numer.astype(BF16), ((0,), (0,)))
            else:
                top_old = top[head]
                top_new = jnp.maximum(top_old, jnp.max(scores, axis=0, keepdims=True))
                fade = jnp.exp(top_old - top_new)
                numer = jnp.exp(scores - top_new)
                total[head] = total[head] * fade + jnp.sum(numer, axis=0, keepdims=True)
                acc[head] = acc[head] * fade + dot(v_h, numer.astype(BF16), ((0,), (0,)))
            top[head] = top_new

    attend(0, True)

    def later_block(d, _):
        attend(d, False)
        return 0

    lax.fori_loop(1, z + 1, later_block, 0)
    for e in range(8):
        cols = slice(e * 128, e * 128 + 128)
        o_s[e] = jnp.concatenate([acc[0, :, cols], acc[1, :, cols]], axis=0).astype(BF16)
        stat_s[e] = jnp.concatenate(
            [top[0, :, cols], total[0, :, cols], top[1, :, cols], total[1, :, cols], jnp.zeros((4, 128), F32)],
            axis=0,
        )
    for e in (4, 3, 5, 2, 6, 1, 7):
        owner = (shifted_seq(s, 0, 8 - e), h)
        remote(o_s.at[e], o_r.at[e], sems.at[8], sems.at[9], owner).start()
        remote(stat_s.at[e], stat_r.at[e], sems.at[10], sems.at[11], owner).start()

    back.wait()
    came_back = back_r[...]
    last = row_1 == 127
    grad_q[...] = jnp.where(last, came_back[0:1, 256:], pltpu.roll(query_grads, 127, 0))
    cross_rows = jnp.where(last, came_back[0:1, :256], pltpu.roll(cross, 127, 0)).astype(BF16)

    def project(c, _):
        cols = pl.ds(pl.multiple_of(c * 512, 512), 512)
        part_s[pl.ds(c, 1)] = dot(cross_rows, w[:, cols], ((1,), (0,))).astype(BF16)[None]
        return 0

    lax.fori_loop(0, 8, project, 0)
    for k in (4, 3, 5, 2, 6, 1, 7):
        owner = lax.rem(h + k, 8)
        remote(part_s.at[owner], part_r.at[k], sems.at[12], sems.at[13], (s, owner)).start()

    others = pl.ds(1, 7)
    neighbour = (shifted_seq(s, 0, 1), h)
    remote(o_s.at[others], o_r.at[others], sems.at[8], sems.at[9], neighbour).wait()
    remote(stat_s.at[others], stat_r.at[others], sems.at[10], sems.at[11], neighbour).wait()
    merged = []
    for head in range(2):
        tops = [(stat_s if e == 0 else stat_r)[e, 2 * head : 2 * head + 1] for e in range(8)]
        totals = [(stat_s if e == 0 else stat_r)[e, 2 * head + 1 : 2 * head + 2] for e in range(8)]
        best = functools.reduce(jnp.maximum, tops)
        fades = [jnp.exp(t - best) for t in tops]
        whole = sum(t * f for t, f in zip(totals, fades))
        summed = sum(
            (o_s if e == 0 else o_r)[e, head * 128 : head * 128 + 128].astype(F32) * fades[e]
            for e in range(8)
        )
        merged.append(jnp.transpose(summed / whole))
    self_out[...] = jnp.concatenate(merged, axis=1).astype(BF16)

    remote(
        part_s.at[others], part_r.at[others], sems.at[12], sems.at[13], (s, lax.rem(h + 1, 8))
    ).wait()
    summed = part_s[pl.ds(h, 1)].reshape(128, 512).astype(F32)
    for k in range(1, 8):
        summed += part_r[k].astype(F32)
    projected[...] = summed.astype(BF16)

    wait_all(gs, gr, 4)
    returned = gr[...].astype(F32)
    chosen = sel_t[...]
    for out, piece in ((grad_k, returned[:, :8]), (grad_v, returned[:, 8:])):
        rows = piece.reshape(512, 256).astype(BF16)
        out[...] = dot(chosen, rows, ((1,), (0,))).astype(BF16).reshape(256, 2, 256)


def shards(sq, sk, sv, cq, store_k, store_v, ids, w, go):
    any_space = pl.BlockSpec(memory_space=pl.ANY)
    vmem = pl.BlockSpec(memory_space=pltpu.VMEM)
    V = pltpu.VMEM
    dma = pltpu.SemaphoreType.DMA
    return pl.pallas_call(
        body,
        name="retrieval_attention",
        out_shape=(
            jax.ShapeDtypeStruct((128, 256), BF16),
            jax.ShapeDtypeStruct((128, 512), BF16),
            jax.ShapeDtypeStruct((128, 256), F32),
            jax.ShapeDtypeStruct((256, 2, 256), BF16),
            jax.ShapeDtypeStruct((256, 2, 256), BF16),
        ),
        in_specs=[any_space] * 6 + [vmem] + [any_space] * 2,
        out_specs=(vmem,) * 5,
        scratch_shapes=[
            V((8, 256, 256), BF16),
            V((8, 128, 256), BF16),
            V((128, 256), BF16),
            V((256, 2, 256), BF16),
            V((256, 2, 256), BF16),
            V((256, 4096), BF16),
            V((128, 4096), BF16),
            V((512, 512), BF16),
            V((64, 16, 256), BF16),
            V((64, 16, 256), BF16),
            V((64, 16, 256), BF16),
            V((64, 16, 256), BF16),
            V((128, 256), BF16),
            V((32, 256), BF16),
            V((32, 256), BF16),
            V((8, 512), F32),
            V((8, 512), F32),
            V((2, 128, 1024), F32),
            V((2, 1, 1024), F32),
            V((2, 1, 1024), F32),
            V((8, 256, 128), BF16),
            V((8, 256, 128), BF16),
            V((8, 8, 128), F32),
            V((8, 8, 128), F32),
            V((8, 128, 512), BF16),
            V((8, 128, 512), BF16),
            dma((8,)),
            dma((2, 5, Z_CHUNKS)),
            dma((2, 5, Z_CHUNKS)),
            dma((2, 5, Y_CHUNKS)),
            dma((2, 5, Y_CHUNKS)),
            dma((14,)),
        ],
        compiler_params=pltpu.CompilerParams(
            collective_id=0, has_side_effects=True, vmem_limit_bytes=50 << 20
        ),
    )(sq, sk, sv, cq, store_k, store_v, ids.T, w, go)


def solution(mesh):
    by_token = P("seq", "heads")
    by_row = P(None, "seq", "heads")
    return jax.shard_map(
        shards,
        mesh=mesh,
        in_specs=(
            by_token, by_token, by_token, by_token, by_row, by_row, P(), P("heads", None), P("seq", None),
        ),
        out_specs=(by_token, by_token, by_token, by_row, by_row),
        check_vma=False,
    )
```

time: 252 us -> 84.8 us (0.34)
  the two profiles are of different devices: /device:TPU:14 before, /device:TPU:8 now
where the time goes in v1:
time: 84.8 us; the launch traced here: 84.3 us
  Pallas kernels  73.2 us (86%)
  local copies, waits for them, and re-layouts  10.5 us (12%)
    pallas_call x1, Pallas kernels, shards(): pl.pallas_call(body, name='retrieval_attention', out_shape=(jax.ShapeDtyp...  73.2 us
    unnamed x21, local copies, waits for them, and re-layouts  10.5 us

profile of v1, /device:TPU:8, one launch (start us, length us, event | category | flops | bytes accessed | tf_op | source)
XLA Modules:
  0.0 84.3 jit_solution(17767616853575602460)
XLA Ops:
  0.6 0.0 copy-start
  0.6 1.2 %copy-done = bf16[128,4096]{1,0:T(8,128)(2,1)S(1)} copy-done((bf16[128,4096]{1,0:T(8,128)(2,1)S(1)}, bf16[128,4096]{1,0:T(8,128)(2,1)}, u32[]{:S(2)}) %copy-start) | copy-done | bytes 1048600
  1.9 0.0 copy-start.1
  1.9 0.9 %copy-done.1 = bf16[256,2,256]{2,1,0:T(2,128)(2,1)S(1)} copy-done((bf16[256,2,256]{2,1,0:T(2,128)(2,1)S(1)}, bf16[256,2,256]{2,1,0:T(2,128)(2,1)}, u32[]{:S(2)}) %copy-start.1) | copy-done | bytes 262168
  2.8 0.0 copy-start.2
  2.8 0.9 %copy-done.2 = bf16[256,2,256]{2,1,0:T(2,128)(2,1)S(1)} copy-done((bf16[256,2,256]{2,1,0:T(2,128)(2,1)S(1)}, bf16[256,2,256]{2,1,0:T(2,128)(2,1)}, u32[]{:S(2)}) %copy-start.2) | copy-done | bytes 262168
  3.8 0.0 copy-start.3
  3.8 0.8 copy-done.3
  4.6 0.0 copy-start.4
  4.6 0.8 copy-done.4
  5.4 0.0 copy-start.5
  5.4 0.8 copy-done.5
  6.3 0.0 copy-start.6
  6.3 0.8 copy-done.6
  7.1 0.0 copy-start.7
  7.1 0.7 copy-done.7
  7.8 73.2 %retrieval_attention.1 = (bf16[128,256]{1,0:T(8,128)(2,1)S(1)}, bf16[128,512]{1,0:T(8,128)(2,1)S(1)}, f32[128,256]{1,0:T(8,128)S(1)}, bf16[256,2,256]{2,1,0:T(2,128)(2,1)S(1)}, bf16[256,2,256]{2,1,0:T(2,128)(2,1)S(1)}) custom-call(bf16[128,256]{1,0:T(8,128)(2,1)S(1)} %copy-done.3, bf16[128,256]{1,0:T(8,128)(2,1)S(1)} %copy-done.4, ...), custom_call_target="tpu_custom_call" | custom-call | tf_op jit(solution)/shard_map/retrieval_attention/pallas_call | solution.py:352
  81.0 0.6 copy.19
  81.6 0.7 copy.20
  82.3 0.7 copy.21
  82.9 0.7 copy.22
  83.6 0.7 copy.23
Async XLA Ops:
  0.6 1.2 %copy-start = (bf16[128,4096]{1,0:T(8,128)(2,1)S(1)}, bf16[128,4096]{1,0:T(8,128)(2,1)}, u32[]{:S(2)}) copy-start(bf16[128,4096]{1,0:T(8,128)(2,1)} %go_in.1) | copy-start | bytes 3145732
  1.9 0.9 %copy-start.1 = (bf16[256,2,256]{2,1,0:T(2,128)(2,1)S(1)}, bf16[256,2,256]{2,1,0:T(2,128)(2,1)}, u32[]{:S(2)}) copy-start(bf16[256,2,256]{2,1,0:T(2,128)(2,1)} %stk_in.1) | copy-start | bytes 786436
  2.8 0.9 %copy-start.2 = (bf16[256,2,256]{2,1,0:T(2,128)(2,1)S(1)}, bf16[256,2,256]{2,1,0:T(2,128)(2,1)}, u32[]{:S(2)}) copy-start(bf16[256,2,256]{2,1,0:T(2,128)(2,1)} %stv_in.1) | copy-start | bytes 786436
  3.8 0.8 copy-start.3
  4.6 0.8 copy-start.4
  5.4 0.8 copy-start.5
  6.3 0.8 copy-start.6
  7.1 0.7 copy-start.7

commit v2 on v1

v2 whole, which is shorter than its diff:
```python
import functools
import math

import jax
import jax.numpy as jnp
from jax import lax
from jax.experimental import pallas as pl
from jax.experimental.pallas import tpu as pltpu
from jax.sharding import PartitionSpec as P

MESH = pl.DeviceIdType.MESH
BF16 = jnp.bfloat16
F32 = jnp.float32
HEAD_DIM = 128
SCALE = 1.0 / math.sqrt(HEAD_DIM)
LOW = -1e30
CHUNKS = 2


def dot(a, b, dims):
    return lax.dot_general(a, b, (dims, ((), ())), preferred_element_type=F32)


def iota(shape, axis):
    return lax.broadcasted_iota(jnp.int32, shape, axis)


def remote(src, dst, send_sem, recv_sem, device):
    return pltpu.make_async_remote_copy(
        src_ref=src,
        dst_ref=dst,
        send_sem=send_sem,
        recv_sem=recv_sem,
        device_id=device,
        device_id_type=MESH,
    )


def shifted_seq(s, dz, dy):
    return lax.rem(s // 8 + dz, 8) * 8 + lax.rem(lax.rem(s, 8) + dy, 8)


def far_first(i):
    return lax.rem(4 + (1 - 2 * lax.rem(i, 2)) * ((i + 1) // 2), 8)


class Ring:
    def __init__(self, own, buf, send_sem, recv_sem, right, left):
        self.own = own
        self.buf, self.send_sem, self.recv_sem = buf, send_sem, recv_sem
        self.right, self.left = right, left
        self.rows = buf.shape[1] // CHUNKS

    def copy(self, step, rightward, chunk):
        source, target = (step - 1, step) if rightward else ((9 - step) % 8, 8 - step)
        rows = pl.ds(chunk * self.rows, self.rows)
        return remote(
            self.buf.at[source, rows],
            self.buf.at[target, rows],
            self.send_sem.at[int(rightward), step, chunk],
            self.recv_sem.at[int(rightward), step, chunk],
            self.right if rightward else self.left,
        )

    def moves(self, step):
        return [
            (rightward, chunk)
            for chunk in range(CHUNKS)
            for rightward in (True, False)
            if step < 4 or (chunk < CHUNKS // 2) == rightward
        ]

    def finish(self):
        for rightward, chunk in self.moves(4):
            self.copy(4, rightward, chunk).wait_recv()
        for rightward, chunk in self.moves(3):
            if (rightward, chunk) not in self.moves(4):
                self.copy(3, rightward, chunk).wait_recv()

    def finish_sends(self):
        for step in range(1, 5):
            for rightward, chunk in self.moves(step):
                self.copy(step, rightward, chunk).wait_send()


def run_step(rings, step):
    for rightward, chunk in rings[0].moves(step):
        for ring in rings:
            if step > 1:
                ring.copy(step - 1, rightward, chunk).wait_recv()
            ring.copy(step, rightward, chunk).start()


def body(
    sq_in, sk_in, sv_in, cq_in, stk_in, stv_in, idt, w_in, go_in,
    self_out, projected, grad_q, grad_k, grad_v,
    zr, yr, cq, stk, stv, w, go,
    sel_t, sb, rb, gs, gr, gc, shift_s, shift_r, back_s, back_r,
    acc, top, total, oy_s, oy_r, sy_s, sy_r, oz_s, oz_r, sz_s, sz_r, part_s, part_r, pair_s, pair_r, edge_r,
    so_v, pr_v, dq_v, dk_v, dv_v,
    load_sem, z_ss, z_rs, y_ss, y_rs, oz_ss, oz_rs, sz_ss, sz_rs, pair_ss, pair_rs, sems, out_sem, plane_sem,
):
    s, h = lax.axis_index("seq"), lax.axis_index("heads")
    z, y = s // 8, lax.rem(s, 8)
    low, high = pl.ds(0, 128), pl.ds(128, 128)
    k_rows, v_rows, q_rows = pl.ds(0, 128), pl.ds(128, 128), pl.ds(256, 128)

    barrier = pltpu.get_barrier_semaphore()

    def greet_lines(k, _):
        step = far_first(k)
        for device in ((shifted_seq(s, step, 0), h), (shifted_seq(s, 0, step), h)):
            pl.semaphore_signal(barrier, inc=1, device_id=device, device_id_type=MESH)
        return 0

    lax.fori_loop(0, 7, greet_lines, 0)
    x, core = h // 2, lax.rem(h, 2)
    sibling = (s, h + 1 - 2 * core)

    def same_core(row, dx):
        return (row, lax.rem(x + dx, 4) * 2 + core)

    near = [sibling] + [same_core(s, dx) for dx in (1, 2, 3)]
    near += [same_core(row, dx) for row in (lax.rem(s + 1, 64), lax.rem(s + 63, 64)) for dx in range(4)]
    for device in near:
        pl.semaphore_signal(barrier, inc=1, device_id=device, device_id_type=MESH)

    def load(i, src, dst):
        return pltpu.make_async_copy(src, dst, load_sem.at[i])

    z_own = (sk_in.at[:, low], sv_in.at[:, low], sq_in.at[:, high])
    y_own = (sk_in.at[:, high], sv_in.at[:, high], sq_in.at[:, low])
    parts = (k_rows, v_rows, q_rows)
    loads = [load(0, stk_in, stk), load(1, stv_in, stv), load(2, go_in, go), load(3, w_in, w), load(4, cq_in, cq)]
    loads += [load(5 + i, z_own[i], zr.at[0, parts[i]]) for i in range(3)]
    loads += [load(8 + i, y_own[i], yr.at[0, parts[i]]) for i in range(3)]
    for copy in loads[5:] + loads[:5]:
        copy.start()

    def halves(own):
        return [ref.at[pl.ds(half, 64)] for ref in own for half in (0, 64)]


    pl.semaphore_wait(barrier, 26)

    def greet_plane(k, _):
        device = (shifted_seq(s, far_first(k), 0), h)
        pl.semaphore_signal(plane_sem, inc=1, device_id=device, device_id_type=MESH)
        return 0

    lax.fori_loop(0, 7, greet_plane, 0)
    rings = (
        Ring(halves(z_own), zr, z_ss, z_rs, (shifted_seq(s, 1, 0), h), (shifted_seq(s, 7, 0), h)),
        Ring(halves(y_own), yr, y_ss, y_rs, (shifted_seq(s, 0, 1), h), (shifted_seq(s, 0, 7), h)),
    )
    for copy in loads[5:]:
        copy.wait()
    run_step(rings, 1)

    ids = idt[...].astype(F32)
    first_id = jnp.broadcast_to(ids[0:1], (128, 128)).astype(BF16)
    second_id = jnp.broadcast_to(ids[1:2], (128, 128)).astype(BF16)
    sub, lane = iota((512, 128), 0), iota((512, 128), 1)
    span_of = (lane == (((sub >> 2) + 127) & 127)).astype(F32).astype(BF16)
    picked = jnp.where(
        (sub & 2) == 0,
        dot(span_of, first_id, ((1,), (1,))),
        dot(span_of, second_id, ((1,), (1,))),
    )
    wanted = picked * 2.0 + (sub & 1).astype(F32)
    lane_f = lane.astype(F32)
    sel = jnp.concatenate(
        [jnp.where(wanted == lane_f + 128.0 * c, 1.0, 0.0).astype(BF16) for c in range(4)], axis=1
    )
    loads[0].wait()
    keys_out = dot(sel, stk[...].reshape(512, 256), ((1,), (0,)))
    loads[1].wait()
    values_out = dot(sel, stv[...].reshape(512, 256), ((1,), (0,)))
    sb[...] = jnp.concatenate(
        [keys_out.reshape(64, 8, 256), values_out.reshape(64, 8, 256)], axis=1
    ).astype(BF16)
    rb[pl.ds(s, 1)] = sb[pl.ds(s, 1)]


    def start_all(source, target, which):
        def one(k, _):
            to = shifted_seq(s, far_first(k // 8), far_first(lax.rem(k, 8)))
            remote(source.at[to], target.at[s], sems.at[which], sems.at[which + 1], (to, h)).start()
            return 0

        lax.fori_loop(0, 63, one, 0)

    def wait_all(source, target, which):
        rows = pl.ds(0, 63)
        remote(
            source.at[rows],
            target.at[rows],
            sems.at[which],
            sems.at[which + 1],
            (shifted_seq(s, 0, 1), h),
        ).wait()

    after = (lax.rem(s + 1, 64), h)
    before = (lax.rem(s + 63, 64), h)

    pl.semaphore_wait(plane_sem, 7)
    start_all(sb, rb, 2)

    run_step(rings, 2)


    run_step(rings, 3)

    loads[2].wait()
    loads[3].wait()
    gc[...] = dot(go[...], w[...], ((1,), (1,))).astype(BF16)
    loads[4].wait()
    shift_s[pl.ds(0, 16)] = cq[pl.ds(112, 16)]
    shift_s[pl.ds(16, 16)] = gc[pl.ds(112, 16)]
    ahead = remote(shift_s, shift_r, sems.at[0], sems.at[1], after)
    ahead.start()

    run_step(rings, 4)

    sub_w, lane_w = iota((128, 512), 0), iota((128, 512), 1)
    span_row = (sub_w == (((lane_w >> 2) + 127) & 127)).astype(F32).astype(BF16)
    lane_8 = iota((8, 512), 1)
    picked_row = jnp.where(
        (lane_8 & 2) == 0,
        dot(first_id[0:8], span_row, ((1,), (0,))),
        dot(second_id[0:8], span_row, ((1,), (0,))),
    )
    wanted_row = (picked_row * 2.0 + (lane_8 & 1).astype(F32))[0:1]
    sel_t[...] = jnp.where(iota((512, 512), 0).astype(F32) == wanted_row, 1.0, 0.0).astype(BF16)

    ahead.wait()
    row_1 = iota((128, 256), 0)
    shifted_in = shift_r[...].astype(F32)
    queries = jnp.where(
        row_1 == 0, shifted_in[15:16], pltpu.roll(cq[...].astype(F32), 1, 0)
    ).astype(BF16)
    place = row_1 + s * 128
    unmatched = (place >= 1) & (place < 64)
    grads = jnp.where(row_1 == 0, shifted_in[31:32], pltpu.roll(gc[...].astype(F32), 1, 0))
    grads = jnp.where(unmatched, 0.0, grads).astype(BF16)
    wait_all(sb, rb, 2)
    got = rb[...].astype(F32)
    near_keys = got[:, :8].reshape(512, 256).astype(BF16)
    near_values = got[:, 8:].reshape(512, 256).astype(BF16)
    mine = ((iota((512, 128), 0) & 4) != 0) == (iota((512, 128), 1) >= 64)
    outs, query_grads, key_grads, value_grads = [], [], [], []
    for head in range(2):
        cols = slice(head * 128, head * 128 + 128)
        k_h, v_h, q_h, g_h = near_keys[:, cols], near_values[:, cols], queries[:, cols], grads[:, cols]
        scores = jnp.where(mine, dot(k_h, q_h, ((1,), (1,))) * SCALE, LOW)
        numer = jnp.exp(scores - jnp.max(scores, axis=0, keepdims=True))
        probs = numer / jnp.sum(numer, axis=0, keepdims=True)
        weights = probs.astype(BF16)
        outs.append(dot(weights, v_h, ((0,), (0,))))
        grad_probs = dot(v_h, g_h, ((1,), (1,)))
        centre = jnp.sum(probs * grad_probs, axis=0, keepdims=True)
        grad_weights = (probs * (grad_probs - centre)).astype(BF16)
        query_grads.append(dot(grad_weights, k_h, ((0,), (0,))) * SCALE)
        key_grads.append(dot(grad_weights, q_h, ((1,), (0,))) * SCALE)
        value_grads.append(dot(weights, g_h, ((1,), (0,))))
    key_grads = jnp.concatenate(key_grads, axis=1).reshape(64, 8, 256)
    value_grads = jnp.concatenate(value_grads, axis=1).reshape(64, 8, 256)
    gs[...] = jnp.concatenate([key_grads, value_grads], axis=1).astype(BF16)
    gr[pl.ds(s, 1)] = gs[pl.ds(s, 1)]
    cross = jnp.where(unmatched, 0.0, jnp.concatenate(outs, axis=1))
    query_grads = jnp.concatenate(query_grads, axis=1)
    back_s[...] = query_grads[0:8]
    back = remote(back_s, back_r, sems.at[4], sems.at[5], before)
    back.start()
    start_all(gs, gr, 6)

    cross_rows = cross.astype(BF16)

    def project(dx, half):
        column = (lax.rem(x + dx, 4) * 2 + half) * 512
        return dot(cross_rows, w[:, pl.ds(pl.multiple_of(column, 512), 512)], ((1,), (0,)))

    def to_sibling(dx):
        return remote(pair_s.at[dx], pair_r.at[dx], pair_ss.at[dx], pair_rs.at[dx], sibling)

    for dx in (2, 1, 3, 0):
        pair_s[dx] = project(dx, 1 - core).astype(BF16)
        to_sibling(dx).start()
    for dx in (2, 1, 3, 0):
        own_part = project(dx, core)
        to_sibling(dx).wait_recv()
        part_s[dx] = (own_part + pair_r[dx].astype(F32)).astype(BF16)
        if dx:
            remote(part_s.at[dx], part_r.at[dx], sems.at[12], sems.at[13], same_core(s, dx)).start()
        edge = part_s.at[dx, pl.ds(0, 16)]
        remote(edge, edge_r.at[dx], sems.at[14], sems.at[15], same_core(before[0], dx)).start()

    for ring in rings:
        ring.finish()
    q_low = yr[:, q_rows].reshape(1024, 128)

    def keys_of(d, first):
        k_h, v_h = zr[pl.ds(d, 1), k_rows].reshape(128, 128), zr[pl.ds(d, 1), v_rows].reshape(128, 128)
        scores = dot(k_h, q_low, ((1,), (1,))) * SCALE
        if first:
            key, query = iota((128, 1024), 0), iota((128, 1024), 1)
            block = query >> 7
            allowed = ((block == 0) & (key <= query)) | (block > y)
            scores = jnp.where(allowed, scores, LOW)
            top_new = jnp.max(scores, axis=0, keepdims=True)
            numer = jnp.where(allowed, jnp.exp(scores - top_new), 0.0)
            total[...] = jnp.sum(numer, axis=0, keepdims=True)
            acc[...] = dot(v_h, numer.astype(BF16), ((0,), (0,)))
        else:
            top_old = top[...]
            top_new = jnp.maximum(top_old, jnp.max(scores, axis=0, keepdims=True))
            fade = jnp.exp(top_old - top_new)
            numer = jnp.exp(scores - top_new)
            total[...] = total[...] * fade + jnp.sum(numer, axis=0, keepdims=True)
            acc[...] = acc[...] * fade + dot(v_h, numer.astype(BF16), ((0,), (0,)))
        top[...] = top_new

    keys_of(0, True)

    def later_keys(d, _):
        keys_of(d, False)
        return 0

    lax.fori_loop(1, z + 1, later_keys, 0)
    pad = jnp.zeros((6, 128), F32)
    for e in range(8):
        cols = slice(e * 128, e * 128 + 128)
        oy_s[e] = acc[:, cols].astype(BF16)
        sy_s[e] = jnp.concatenate([top[:, cols], total[:, cols], pad], axis=0)
    for e in (4, 3, 5, 2, 6, 1, 7):
        owner = (shifted_seq(s, 0, 8 - e), h)
        remote(oy_s.at[e], oy_r.at[e], sems.at[8], sems.at[9], owner).start()
        remote(sy_s.at[e], sy_r.at[e], sems.at[10], sems.at[11], owner).start()

    k_high = yr[:, k_rows].reshape(1024, 128)
    v_high = yr[:, v_rows].reshape(1024, 128)

    def queries_of(d, first):
        scores = dot(k_high, zr[pl.ds(d, 1), q_rows].reshape(128, 128), ((1,), (1,))) * SCALE
        if first:
            key, query = iota((1024, 128), 0), iota((1024, 128), 1)
            block = key >> 7
            allowed = (key <= query) | ((block >= 1) & (block <= y))
            scores = jnp.where(allowed, scores, LOW)
        best = jnp.max(scores, axis=0, keepdims=True)
        numer = jnp.exp(scores - best)
        whole = jnp.sum(numer, axis=0, keepdims=True)
        out = dot(v_high, numer.astype(BF16), ((0,), (0,)))
        return best, whole, out

    def move_z(d):
        owner = (shifted_seq(s, 8 - d, 0), h)
        return (
            remote(oz_s.at[d], oz_r.at[d], oz_ss.at[d], oz_rs.at[d], owner),
            remote(sz_s.at[d], sz_r.at[d], sz_ss.at[d], sz_rs.at[d], owner),
        )

    def later_queries(d, _):
        best, whole, out = queries_of(d, False)
        oz_s[pl.ds(d, 1)] = out.astype(BF16)[None]
        sz_s[pl.ds(d, 1)] = jnp.concatenate([best, whole, pad], axis=0)[None]
        for copy in move_z(d):
            copy.start()
        return 0

    lax.fori_loop(z + 1, 8, later_queries, 0)
    own_high = queries_of(0, True)

    others = pl.ds(1, 7)
    neighbour = (shifted_seq(s, 0, 1), h)
    remote(oy_s.at[others], oy_r.at[others], sems.at[8], sems.at[9], neighbour).wait()
    remote(sy_s.at[others], sy_r.at[others], sems.at[10], sems.at[11], neighbour).wait()
    stats = [sy_s[0]] + [sy_r[e] for e in range(1, 8)]
    best = functools.reduce(jnp.maximum, [stat[0:1] for stat in stats])
    fades = [jnp.exp(stat[0:1] - best) for stat in stats]
    whole = sum(stat[1:2] * fade for stat, fade in zip(stats, fades))
    summed = oy_s[0].astype(F32) * fades[0]
    for e in range(1, 8):
        summed += oy_r[e].astype(F32) * fades[e]
    out_low = jnp.transpose(summed / whole)

    def merge_z(d, carry):
        best, whole, out = carry
        for copy in move_z(d):
            copy.wait_recv()
        stat = sz_r[pl.ds(d, 1)].reshape(8, 128)
        best_new = jnp.maximum(best, stat[0:1])
        fade, fade_in = jnp.exp(best - best_new), jnp.exp(stat[0:1] - best_new)
        out_in = oz_r[pl.ds(d, 1)].reshape(128, 128).astype(F32)
        return best_new, whole * fade + stat[1:2] * fade_in, out * fade + out_in * fade_in

    best, whole, out = lax.fori_loop(8 - z, 8, merge_z, own_high)
    out_high = jnp.transpose(out / whole)
    so_v[...] = jnp.concatenate([out_low, out_high], axis=1).astype(BF16)
    out_so = pltpu.make_async_copy(so_v, self_out, out_sem.at[1])
    out_so.start()

    three, four = pl.ds(1, 3), pl.ds(0, 4)
    remote(part_s.at[three], part_r.at[three], sems.at[12], sems.at[13], same_core(s, 1)).wait()
    remote(
        part_s.at[four, pl.ds(0, 16)], edge_r.at[four], sems.at[14], sems.at[15], same_core(before[0], 1)
    ).wait()
    for dx in range(4):
        to_sibling(dx).wait_send()
    summed, edge = part_s[0].astype(F32), edge_r[0].astype(F32)
    for dx in range(1, 4):
        summed += part_r[dx].astype(F32)
        edge += edge_r[dx].astype(F32)
    pr_v[...] = jnp.where(
        iota((128, 512), 0) == 127, edge[0:1], pltpu.roll(summed, 127, 0)
    ).astype(BF16)
    out_pr = pltpu.make_async_copy(pr_v, projected, out_sem.at[2])
    out_pr.start()

    back.wait()
    dq_v[...] = jnp.where(row_1 == 127, back_r[0:1], pltpu.roll(query_grads, 127, 0))
    out_dq = pltpu.make_async_copy(dq_v, grad_q, out_sem.at[0])
    out_dq.start()

    def sent_z(d, _):
        for copy in move_z(d):
            copy.wait_send()
        return 0

    lax.fori_loop(z + 1, 8, sent_z, 0)
    for ring in rings:
        ring.finish_sends()

    wait_all(gs, gr, 6)
    returned = gr[...].astype(F32)
    chosen = sel_t[...]
    copies = [out_dq, out_so, out_pr]
    for i, (held, out, piece) in enumerate(
        ((dk_v, grad_k, returned[:, :8]), (dv_v, grad_v, returned[:, 8:]))
    ):
        rows = piece.reshape(512, 256).astype(BF16)
        held[...] = dot(chosen, rows, ((1,), (0,))).astype(BF16).reshape(256, 2, 256)
        copies.append(pltpu.make_async_copy(held, out, out_sem.at[3 + i]))
        copies[-1].start()
    for copy in copies:
        copy.wait()


def hand_over(*refs):
    sources, targets, held, sem = refs[:5], refs[5:10], refs[10:15], refs[15]
    reads = [pltpu.make_async_copy(a, b, sem.at[0, i]) for i, (a, b) in enumerate(zip(sources, held))]
    writes = [pltpu.make_async_copy(a, b, sem.at[1, i]) for i, (a, b) in enumerate(zip(held, targets))]
    for read in reads:
        read.start()
    for read, write in zip(reads, writes):
        read.wait()
        write.start()
    for write in writes:
        write.wait()


def shards(sq, sk, sv, cq, store_k, store_v, ids, w, go):
    any_space = pl.BlockSpec(memory_space=pl.ANY)
    vmem = pl.BlockSpec(memory_space=pltpu.VMEM)
    V = pltpu.VMEM
    dma = pltpu.SemaphoreType.DMA
    shapes = (
        jax.ShapeDtypeStruct((128, 256), BF16),
        jax.ShapeDtypeStruct((128, 512), BF16),
        jax.ShapeDtypeStruct((128, 256), F32),
        jax.ShapeDtypeStruct((256, 2, 256), BF16),
        jax.ShapeDtypeStruct((256, 2, 256), BF16),
    )
    results = pl.pallas_call(
        body,
        name="retrieval_attention",
        out_shape=shapes,
        in_specs=[any_space] * 6 + [vmem] + [any_space] * 2,
        out_specs=(any_space,) * 5,
        scratch_shapes=[
            V((8, 384, 128), BF16),
            V((8, 384, 128), BF16),
            V((128, 256), BF16),
            V((256, 2, 256), BF16),
            V((256, 2, 256), BF16),
            V((256, 4096), BF16),
            V((128, 4096), BF16),
            V((512, 512), BF16),
            V((64, 16, 256), BF16),
            V((64, 16, 256), BF16),
            V((64, 16, 256), BF16),
            V((64, 16, 256), BF16),
            V((128, 256), BF16),
            V((32, 256), BF16),
            V((32, 256), BF16),
            V((8, 256), F32),
            V((8, 256), F32),
            V((128, 1024), F32),
            V((1, 1024), F32),
            V((1, 1024), F32),
            V((8, 128, 128), BF16),
            V((8, 128, 128), BF16),
            V((8, 8, 128), F32),
            V((8, 8, 128), F32),
            V((8, 128, 128), BF16),
            V((8, 128, 128), BF16),
            V((8, 8, 128), F32),
            V((8, 8, 128), F32),
            V((4, 128, 512), BF16),
            V((4, 128, 512), BF16),
            V((4, 128, 512), BF16),
            V((4, 128, 512), BF16),
            V((4, 16, 512), BF16),
            V((128, 256), BF16),
            V((128, 512), BF16),
            V((128, 256), F32),
            V((256, 2, 256), BF16),
            V((256, 2, 256), BF16),
            dma((11,)),
            dma((2, 5, CHUNKS)),
            dma((2, 5, CHUNKS)),
            dma((2, 5, CHUNKS)),
            dma((2, 5, CHUNKS)),
            dma((8,)),
            dma((8,)),
            dma((8,)),
            dma((8,)),
            dma((4,)),
            dma((4,)),
            dma((16,)),
            dma((5,)),
            pltpu.SemaphoreType.REGULAR,
        ],
        compiler_params=pltpu.CompilerParams(
            collective_id=0, has_side_effects=True, vmem_limit_bytes=60 << 20
        ),
    )(sq, sk, sv, cq, store_k, store_v, ids.T, w, go)
    return pl.pallas_call(
        hand_over,
        name="hand_over",
        out_shape=shapes,
        in_specs=[any_space] * 5,
        out_specs=(any_space,) * 5,
        scratch_shapes=[V(shape.shape, shape.dtype) for shape in shapes] + [dma((2, 5))],
        compiler_params=pltpu.CompilerParams(vmem_limit_bytes=60 << 20),
    )(*results)


def solution(mesh):
    by_token = P("seq", "heads")
    by_row = P(None, "seq", "heads")
    return jax.shard_map(
        shards,
        mesh=mesh,
        in_specs=(
            by_token, by_token, by_token, by_token, by_row, by_row, P(), P("heads", None), P("seq", None),
        ),
        out_specs=(by_token, by_token, by_token, by_row, by_row),
        check_vma=False,
    )
```

time: 84.8 us -> 65.1 us (0.77)
  local copies, waits for them, and re-layouts: 10.5 us -> 0 us
  Pallas kernels: 73.2 us -> 64.3 us
    unnamed x21 -> x0, local copies, waits for them, and re-layouts: 10.5 us -> none
    pallas_call x1 -> x2, Pallas kernels: 73.2 us -> 64.3 us  [the longest x1 62.3 us: shards(): pl.pallas_call(body, name='retrieval_attention', out_shape=shapes, in_spe...]
where the time goes in v2:
time: 65.1 us; the launch traced here: 65 us
  Pallas kernels  64.3 us (99%)
    pallas_call x1, Pallas kernels, shards(): pl.pallas_call(body, name='retrieval_attention', out_shape=shapes, in_spe...  62.3 us
    pallas_call x1, Pallas kernels, shards(): pl.pallas_call(hand_over, name='hand_over', out_shape=shapes, in_specs=[a...  1.99 us

profile of v2, /device:TPU:8, one launch (start us, length us, event | category | flops | bytes accessed | tf_op | source)
XLA Modules:
  0.0 65.0 jit_solution(10721464395310409440)
XLA Ops:
  0.6 62.3 %retrieval_attention.1 = (bf16[128,256]{1,0:T(8,128)(2,1)}, bf16[128,512]{1,0:T(8,128)(2,1)}, f32[128,256]{1,0:T(8,128)}, bf16[256,2,256]{2,1,0:T(2,128)(2,1)}, bf16[256,2,256]{2,1,0:T(2,128)(2,1)}) custom-call(bf16[128,256]{1,0:T(8,128)(2,1)} %sq_in.1, bf16[128,256]{1,0:T(8,128)(2,1)} %sk_in.1, bf16[128,256]{1,0:T(8,128)(2,1)} %sv_in.1, ...), custom_call_target="tpu_custom_call" | custom-call | tf_op jit(solution)/shard_map/retrieval_attention/pallas_call | solution.py:474
  63.0 2.0 %hand_over.1 = (bf16[128,256]{1,0:T(8,128)(2,1)}, bf16[128,512]{1,0:T(8,128)(2,1)}, f32[128,256]{1,0:T(8,128)}, bf16[256,2,256]{2,1,0:T(2,128)(2,1)}, bf16[256,2,256]{2,1,0:T(2,128)(2,1)}) custom-call(bf16[128,256]{1,0:T(8,128)(2,1)} %get-tuple-element.10.refs_0_, bf16[128,512]{1,0:T(8,128)(2,1)} %get-tuple-element.11.refs_1_, ...), custom_call_target="tpu_custom_call" | custom-call | tf_op jit(solution)/shard_map/hand_over/pallas_call | solution.py:538

commit v3 on v2

--- a/solution.py
+++ b/solution.py
@@ -44,16 +44,22 @@
     return lax.rem(4 + (1 - 2 * lax.rem(i, 2)) * ((i + 1) // 2), 8)
 
 
+def only(needed, act):
+    if needed is None:
+        act()
+    else:
+        pl.when(needed)(act)
+
+
 class Ring:
-    def __init__(self, own, buf, send_sem, recv_sem, right, left):
-        self.own = own
+    def __init__(self, buf, send_sem, recv_sem, right, left, chunks, needs=None):
         self.buf, self.send_sem, self.recv_sem = buf, send_sem, recv_sem
-        self.right, self.left = right, left
-        self.rows = buf.shape[1] // CHUNKS
+        self.right, self.left, self.chunks = right, left, chunks
+        self.needs = needs or (lambda *move: None)
 
     def copy(self, step, rightward, chunk):
         source, target = (step - 1, step) if rightward else ((9 - step) % 8, 8 - step)
-        rows = pl.ds(chunk * self.rows, self.rows)
+        rows = pl.ds(*self.chunks[chunk])
         return remote(
             self.buf.at[source, rows],
             self.buf.at[target, rows],
@@ -70,25 +76,31 @@
             if step < 4 or (chunk < CHUNKS // 2) == rightward
         ]
 
+    def start(self, step, rightward, chunk):
+        only(self.needs(step, rightward, chunk, True), self.copy(step, rightward, chunk).start)
+
+    def received(self, step, rightward, chunk):
+        only(self.needs(step, rightward, chunk, False), self.copy(step, rightward, chunk).wait_recv)
+
     def finish(self):
-        for rightward, chunk in self.moves(4):
-            self.copy(4, rightward, chunk).wait_recv()
-        for rightward, chunk in self.moves(3):
-            if (rightward, chunk) not in self.moves(4):
-                self.copy(3, rightward, chunk).wait_recv()
+        for move in self.moves(4):
+            self.received(4, *move)
+        for move in self.moves(3):
+            if move not in self.moves(4):
+                self.received(3, *move)
 
     def finish_sends(self):
         for step in range(1, 5):
-            for rightward, chunk in self.moves(step):
-                self.copy(step, rightward, chunk).wait_send()
+            for move in self.moves(step):
+                only(self.needs(step, *move, True), self.copy(step, *move).wait_send)
 
 
 def run_step(rings, step):
-    for rightward, chunk in rings[0].moves(step):
+    for move in rings[0].moves(step):
         for ring in rings:
             if step > 1:
-                ring.copy(step - 1, rightward, chunk).wait_recv()
-            ring.copy(step, rightward, chunk).start()
+                ring.received(step - 1, *move)
+            ring.start(step, *move)
 
 
 def body(
@@ -137,9 +149,6 @@
     for copy in loads[5:] + loads[:5]:
         copy.start()
 
-    def halves(own):
-        return [ref.at[pl.ds(half, 64)] for ref in own for half in (0, 64)]
-
 
     pl.semaphore_wait(barrier, 26)
 
@@ -149,9 +158,22 @@
         return 0
 
     lax.fori_loop(0, 7, greet_plane, 0)
+
+    def needs_z(step, rightward, chunk, sending):
+        at = step - 1 if sending else step
+        if rightward and chunk == 0:
+            return (z >= at) & (z <= 6) if sending else z >= at
+        if not rightward and chunk == 1:
+            return (z + at <= 7) & (z >= 1) if sending else z + at <= 7
+        if rightward:
+            return lax.rem(z + 8 - at, 8) >= 5
+        return lax.rem(z + at, 8) <= 2
+
     rings = (
-        Ring(halves(z_own), zr, z_ss, z_rs, (shifted_seq(s, 1, 0), h), (shifted_seq(s, 7, 0), h)),
-        Ring(halves(y_own), yr, y_ss, y_rs, (shifted_seq(s, 0, 1), h), (shifted_seq(s, 0, 7), h)),
+        Ring(
+            zr, z_ss, z_rs, (shifted_seq(s, 1, 0), h), (shifted_seq(s, 7, 0), h), ((0, 256), (256, 128)), needs_z
+        ),
+        Ring(yr, y_ss, y_rs, (shifted_seq(s, 0, 1), h), (shifted_seq(s, 0, 7), h), ((0, 192), (192, 192))),
     )
     for copy in loads[5:]:
         copy.wait()
@@ -182,13 +204,25 @@
     rb[pl.ds(s, 1)] = sb[pl.ds(s, 1)]
 
 
-    def start_all(source, target, which):
+    def send(source, target, which, dz, dy):
+        to = shifted_seq(s, dz, dy)
+        remote(source.at[to], target.at[s], sems.at[which], sems.at[which + 1], (to, h)).start()
+
+    def start_lines(source, target, which):
         def one(k, _):
-            to = shifted_seq(s, far_first(k // 8), far_first(lax.rem(k, 8)))
-            remote(source.at[to], target.at[s], sems.at[which], sems.at[which + 1], (to, h)).start()
+            step = far_first(k)
+            send(source, target, which, step, 0)
+            send(source, target, which, 0, step)
             return 0
 
-        lax.fori_loop(0, 63, one, 0)
+        lax.fori_loop(0, 7, one, 0)
+
+    def start_rest(source, target, which):
+        def one(k, _):
+            send(source, target, which, far_first(k // 7), far_first(lax.rem(k, 7)))
+            return 0
+
+        lax.fori_loop(0, 49, one, 0)
 
     def wait_all(source, target, which):
         rows = pl.ds(0, 63)
@@ -203,8 +237,9 @@
     after = (lax.rem(s + 1, 64), h)
     before = (lax.rem(s + 63, 64), h)
 
+    start_lines(sb, rb, 2)
     pl.semaphore_wait(plane_sem, 7)
-    start_all(sb, rb, 2)
+    start_rest(sb, rb, 2)
 
     run_step(rings, 2)
 
@@ -272,7 +307,8 @@
     back_s[...] = query_grads[0:8]
     back = remote(back_s, back_r, sems.at[4], sems.at[5], before)
     back.start()
-    start_all(gs, gr, 6)
+    start_rest(gs, gr, 6)
+    start_lines(gs, gr, 6)
 
     cross_rows = cross.astype(BF16)
 

time: 65.1 us -> 63.7 us (0.978)
  Pallas kernels: 64.3 us -> 62.9 us
    pallas_call x1, Pallas kernels: 62.3 us -> 60.9 us  [shards(): pl.pallas_call(body, name='retrieval_attention', out_shape=shapes, in_spe...]
where the time goes in v3:
time: 63.7 us; the launch traced here: 63.6 us
  Pallas kernels  62.9 us (99%)
  between operations  0.64 us (1%)
    pallas_call x1, Pallas kernels, shards(): pl.pallas_call(body, name='retrieval_attention', out_shape=shapes, in_spe...  60.9 us
    pallas_call x1, Pallas kernels, shards(): pl.pallas_call(hand_over, name='hand_over', out_shape=shapes, in_specs=[a...  1.99 us

profile of v3, /device:TPU:8, one launch (start us, length us, event | category | flops | bytes accessed | tf_op | source)
XLA Modules:
  0.0 63.6 jit_solution(13889664339264952644)
XLA Ops:
  0.6 60.9 %retrieval_attention.1 = (bf16[128,256]{1,0:T(8,128)(2,1)}, bf16[128,512]{1,0:T(8,128)(2,1)}, f32[128,256]{1,0:T(8,128)}, bf16[256,2,256]{2,1,0:T(2,128)(2,1)}, bf16[256,2,256]{2,1,0:T(2,128)(2,1)}) custom-call(bf16[128,256]{1,0:T(8,128)(2,1)} %sq_in.1, bf16[128,256]{1,0:T(8,128)(2,1)} %sk_in.1, bf16[128,256]{1,0:T(8,128)(2,1)} %sv_in.1, ...), custom_call_target="tpu_custom_call" | custom-call | tf_op jit(solution)/shard_map/retrieval_attention/pallas_call | solution.py:510
  61.6 2.0 %hand_over.1 = (bf16[128,256]{1,0:T(8,128)(2,1)}, bf16[128,512]{1,0:T(8,128)(2,1)}, f32[128,256]{1,0:T(8,128)}, bf16[256,2,256]{2,1,0:T(2,128)(2,1)}, bf16[256,2,256]{2,1,0:T(2,128)(2,1)}) custom-call(bf16[128,256]{1,0:T(8,128)(2,1)} %get-tuple-element.10.refs_0_, bf16[128,512]{1,0:T(8,128)(2,1)} %get-tuple-element.11.refs_1_, ...), custom_call_target="tpu_custom_call" | custom-call | tf_op jit(solution)/shard_map/hand_over/pallas_call | solution.py:574

commit v4 on v3

--- a/solution.py
+++ b/solution.py
@@ -407,35 +407,6 @@
     lax.fori_loop(z + 1, 8, later_queries, 0)
     own_high = queries_of(0, True)
 
-    others = pl.ds(1, 7)
-    neighbour = (shifted_seq(s, 0, 1), h)
-    remote(oy_s.at[others], oy_r.at[others], sems.at[8], sems.at[9], neighbour).wait()
-    remote(sy_s.at[others], sy_r.at[others], sems.at[10], sems.at[11], neighbour).wait()
-    stats = [sy_s[0]] + [sy_r[e] for e in range(1, 8)]
-    best = functools.reduce(jnp.maximum, [stat[0:1] for stat in stats])
-    fades = [jnp.exp(stat[0:1] - best) for stat in stats]
-    whole = sum(stat[1:2] * fade for stat, fade in zip(stats, fades))
-    summed = oy_s[0].astype(F32) * fades[0]
-    for e in range(1, 8):
-        summed += oy_r[e].astype(F32) * fades[e]
-    out_low = jnp.transpose(summed / whole)
-
-    def merge_z(d, carry):
-        best, whole, out = carry
-        for copy in move_z(d):
-            copy.wait_recv()
-        stat = sz_r[pl.ds(d, 1)].reshape(8, 128)
-        best_new = jnp.maximum(best, stat[0:1])
-        fade, fade_in = jnp.exp(best - best_new), jnp.exp(stat[0:1] - best_new)
-        out_in = oz_r[pl.ds(d, 1)].reshape(128, 128).astype(F32)
-        return best_new, whole * fade + stat[1:2] * fade_in, out * fade + out_in * fade_in
-
-    best, whole, out = lax.fori_loop(8 - z, 8, merge_z, own_high)
-    out_high = jnp.transpose(out / whole)
-    so_v[...] = jnp.concatenate([out_low, out_high], axis=1).astype(BF16)
-    out_so = pltpu.make_async_copy(so_v, self_out, out_sem.at[1])
-    out_so.start()
-
     three, four = pl.ds(1, 3), pl.ds(0, 4)
     remote(part_s.at[three], part_r.at[three], sems.at[12], sems.at[13], same_core(s, 1)).wait()
     remote(
@@ -458,19 +429,10 @@
     out_dq = pltpu.make_async_copy(dq_v, grad_q, out_sem.at[0])
     out_dq.start()
 
-    def sent_z(d, _):
-        for copy in move_z(d):
-            copy.wait_send()
-        return 0
-
-    lax.fori_loop(z + 1, 8, sent_z, 0)
-    for ring in rings:
-        ring.finish_sends()
-
     wait_all(gs, gr, 6)
     returned = gr[...].astype(F32)
     chosen = sel_t[...]
-    copies = [out_dq, out_so, out_pr]
+    copies = [out_dq, out_pr]
     for i, (held, out, piece) in enumerate(
         ((dk_v, grad_k, returned[:, :8]), (dv_v, grad_v, returned[:, 8:]))
     ):
@@ -478,7 +440,46 @@
         held[...] = dot(chosen, rows, ((1,), (0,))).astype(BF16).reshape(256, 2, 256)
         copies.append(pltpu.make_async_copy(held, out, out_sem.at[3 + i]))
         copies[-1].start()
-    for copy in copies:
+
+    others = pl.ds(1, 7)
+    neighbour = (shifted_seq(s, 0, 1), h)
+    remote(oy_s.at[others], oy_r.at[others], sems.at[8], sems.at[9], neighbour).wait()
+    remote(sy_s.at[others], sy_r.at[others], sems.at[10], sems.at[11], neighbour).wait()
+    stats = [sy_s[0]] + [sy_r[e] for e in range(1, 8)]
+    best = functools.reduce(jnp.maximum, [stat[0:1] for stat in stats])
+    fades = [jnp.exp(stat[0:1] - best) for stat in stats]
+    whole = sum(stat[1:2] * fade for stat, fade in zip(stats, fades))
+    summed = oy_s[0].astype(F32) * fades[0]
+    for e in range(1, 8):
+        summed += oy_r[e].astype(F32) * fades[e]
+    out_low = jnp.transpose(summed / whole)
+
+    def merge_z(d, carry):
+        best, whole, out = carry
+        for copy in move_z(d):
+            copy.wait_recv()
+        stat = sz_r[pl.ds(d, 1)].reshape(8, 128)
+        best_new = jnp.maximum(best, stat[0:1])
+        fade, fade_in = jnp.exp(best - best_new), jnp.exp(stat[0:1] - best_new)
+        out_in = oz_r[pl.ds(d, 1)].reshape(128, 128).astype(F32)
+        return best_new, whole * fade + stat[1:2] * fade_in, out * fade + out_in * fade_in
+
+    best, whole, out = lax.fori_loop(8 - z, 8, merge_z, own_high)
+    out_high = jnp.transpose(out / whole)
+    so_v[...] = jnp.concatenate([out_low, out_high], axis=1).astype(BF16)
+    out_so = pltpu.make_async_copy(so_v, self_out, out_sem.at[1])
+    out_so.start()
+
+    def sent_z(d, _):
+        for copy in move_z(d):
+            copy.wait_send()
+        return 0
+
+    lax.fori_loop(z + 1, 8, sent_z, 0)
+    for ring in rings:
+        ring.finish_sends()
+
+    for copy in copies + [out_so]:
         copy.wait()
 
 

time: 63.7 us -> 62.9 us (0.987)
  Pallas kernels: 62.9 us -> 62.1 us
    pallas_call x1, Pallas kernels: 60.9 us -> 60.1 us  [shards(): pl.pallas_call(body, name='retrieval_attention', out_shape=shapes, in_spe...]
where the time goes in v4:
time: 62.9 us; the launch traced here: 62.7 us
  Pallas kernels  62.1 us (99%)
  between operations  0.64 us (1%)
    pallas_call x1, Pallas kernels, shards(): pl.pallas_call(body, name='retrieval_attention', out_shape=shapes, in_spe...  60.1 us
    pallas_call x1, Pallas kernels, shards(): pl.pallas_call(hand_over, name='hand_over', out_shape=shapes, in_specs=[a...  1.99 us

profile of v4, /device:TPU:8, one launch (start us, length us, event | category | flops | bytes accessed | tf_op | source)
XLA Modules:
  0.0 62.7 jit_solution(14363879680025771343)
XLA Ops:
  0.6 60.1 %retrieval_attention.1 = (bf16[128,256]{1,0:T(8,128)(2,1)}, bf16[128,512]{1,0:T(8,128)(2,1)}, f32[128,256]{1,0:T(8,128)}, bf16[256,2,256]{2,1,0:T(2,128)(2,1)}, bf16[256,2,256]{2,1,0:T(2,128)(2,1)}) custom-call(bf16[128,256]{1,0:T(8,128)(2,1)} %sq_in.1, bf16[128,256]{1,0:T(8,128)(2,1)} %sk_in.1, bf16[128,256]{1,0:T(8,128)(2,1)} %sv_in.1, ...), custom_call_target="tpu_custom_call" | custom-call | tf_op jit(solution)/shard_map/retrieval_attention/pallas_call | solution.py:511
  60.7 2.0 %hand_over.1 = (bf16[128,256]{1,0:T(8,128)(2,1)}, bf16[128,512]{1,0:T(8,128)(2,1)}, f32[128,256]{1,0:T(8,128)}, bf16[256,2,256]{2,1,0:T(2,128)(2,1)}, bf16[256,2,256]{2,1,0:T(2,128)(2,1)}) custom-call(bf16[128,256]{1,0:T(8,128)(2,1)} %get-tuple-element.10.refs_0_, bf16[128,512]{1,0:T(8,128)(2,1)} %get-tuple-element.11.refs_1_, ...), custom_call_target="tpu_custom_call" | custom-call | tf_op jit(solution)/shard_map/hand_over/pallas_call | solution.py:575
